TPU v7x, 128 devices: a whole 4x4x4 slice. The times are simulated.
128 devices in a mesh: rows: 32 (over z, y, core), cols: 4 (over x).
Axes of the slice: x: 4, y: 4, z: 4, core: 2. Of those that a mesh axis runs over, the one named last changes fastest.
Arguments:
- basis: float32 [64, 262144], P('cols', 'rows'), may hold values from -450 to 450
- blocks: bfloat16 [1024, 4, 256, 256], P('rows'), may hold values from -16 to 1, as said below
- far_cols: int32 [1024], P('rows'), may hold values from 0 to 1023, as said below
Outputs:
- basis_out: float32 [64, 262144], P('cols', 'rows')
- ritz: float32 [64, 64], P(None, 'cols')
Inputs may be any that keep to these rules, and one draw needn't show every extreme that they name: Off-diagonal entries are positive; each diagonal entry of a diagonal block is minus the sum of the other entries of its row over the four blocks, rounded to bfloat16. `far_cols`: the block rows of one device name at most 2 far columns among the block rows of any one device; the block rows of some device are named by exactly 2 block rows of every device.
All inputs are finite; a program needn't handle non-finite values.
Results may differ from a plain program's by a relative error of at most 0.0036.
Values may be sent and summed in bfloat16 or wider, within the bound.
No kernel may reach another device: no remote copies, remote signals or barrier semaphores. Data moves between devices by JAX's collectives and lax.ppermute only.
A program may use at most 128 MiB of HBM per device.

v0:
```python
import jax
import jax.numpy as jnp
from jax import lax
from jax.sharding import PartitionSpec as P

ITERS = 4


def with_halo(block, sides, width):
    for axis, dim in sides:
        count = lax.axis_size(axis)
        forward = [(i, i + 1) for i in range(count - 1)]
        forward.append((count - 1, 0))
        backward = [(target, source) for source, target in forward]
        low = lax.ppermute(
            lax.slice_in_dim(block, block.shape[dim] - width, None, axis=dim), axis, forward
        )
        high = lax.ppermute(lax.slice_in_dim(block, 0, width, axis=dim), axis, backward)
        block = jnp.concatenate([low, block, high], axis=dim)
    return block


def block_product(pieces, blocks, position):
    return jnp.einsum(
        "jbt,bst->jbs", pieces, blocks[:, position], preferred_element_type=jnp.float32
    )


def body(basis, blocks, far_cols):
    width = basis.shape[0]
    block_rows = blocks.shape[0]
    block_size = blocks.shape[2]
    row_devices = lax.axis_size("rows")
    total_states = block_rows * block_size * row_devices
    modes = width * lax.axis_size("cols")
    highest = lax.Precision.HIGHEST

    def apply_generator(iterate_bf):
        shaped = iterate_bf.reshape(width, block_rows, block_size)
        result = block_product(shaped, blocks, 0)
        empty = jnp.zeros((width, block_rows, block_size), jnp.bfloat16)
        piece = lax.all_gather(shaped, "rows", axis=1, tiled=True)
        inside = jnp.logical_and(far_cols >= 0, far_cols < piece.shape[1])
        taken = jnp.take(piece, jnp.clip(far_cols, 0, piece.shape[1] - 1), axis=1)
        remote = jnp.where(inside[None, :, None], taken, empty)
        extended = with_halo(shaped, (("rows", 1),), 1)
        result = result + block_product(extended[:, :-2], blocks, 1)
        result = result + block_product(extended[:, 2:], blocks, 2)
        result = result + block_product(remote, blocks, 3)
        return result.reshape(width, block_rows * block_size)

    iterate = basis
    for step in range(ITERS):
        iterate = iterate + 0.2 * apply_generator(iterate.astype(jnp.bfloat16))
    whole_iterate = lax.all_gather(iterate, "cols", axis=0, tiled=True)
    contract = (((1,), (1,)), ((), ()))
    gram_part = lax.dot_general(whole_iterate, iterate, contract, precision=highest)
    column_start = lax.axis_index("cols") * width
    gram_mine = lax.psum(gram_part, "rows")
    gram = lax.all_gather(gram_mine, "cols", axis=1, tiled=True) / total_states
    applied = apply_generator(iterate.astype(jnp.bfloat16))
    product_part = lax.dot_general(whole_iterate, applied, contract, precision=highest)
    product_mine = lax.psum(product_part, "rows")
    product = lax.all_gather(product_mine, "cols", axis=1, tiled=True) / total_states
    factor = jnp.linalg.cholesky(gram)
    identity_square = jnp.eye(modes, dtype=factor.dtype)
    inverse_factor = lax.linalg.triangular_solve(
        factor, identity_square, left_side=True, lower=True
    )
    own_rows = lax.dynamic_slice_in_dim(inverse_factor, column_start, width, 0)
    basis_out = jnp.dot(own_rows, whole_iterate, precision=highest)
    left_part = jnp.dot(inverse_factor, product, precision=highest)
    ritz_whole = jnp.dot(left_part, inverse_factor.T, precision=highest)
    ritz = lax.dynamic_slice_in_dim(ritz_whole, column_start, width, 1)
    return (basis_out, ritz)


def solution(mesh):
    in_specs = (P("cols", "rows"), P("rows", None, None, None), P("rows"))
    out_specs = (P("cols", "rows"), P(None, "cols"))
    return jax.shard_map(body, mesh=mesh, in_specs=in_specs, out_specs=out_specs, check_vma=False)
```

profile of v0, /device:TPU:0, one launch (start us, length us, event | category | flops | bytes accessed | tf_op | source)
XLA Modules:
  0.0 539.1 jit_solution(13265493274930220181)
XLA Ops:
  9.8 6.0 %collective-permute-start.1 = (bf16[16,1,256]{2,0,1:T(8,128)(2,1)S(1)}, bf16[16,1,256]{2,0,1:T(8,128)(2,1)S(1)}, u32[]{:S(2)}, u32[]{:S(2)}) collective-permute-start(bf16[16,1,256]{2,0,1:T(8,128)(2,1)S(1)} %get-tuple-element.23), channel_id=1, source_target_pairs={{4,0},{8,4},{12,8},{16,12},{20,16},{24,20},{28,24},{32,28},{36,32}... | collective-permute-start | bytes 24584 | tf_op jit(solution)/shard_map/ppermute | solution.py:18
  19.9 3.6 fusion.84
  23.5 3.5 fusion.81
  27.0 39.3 %all-gather.7.cloned.1.call-done = bf16[16,1024,256]{2,0,1:T(8,128)(2,1)} async-done(((bf16[16,32,256]{2,0,1:T(8,128)(2,1)}), bf16[16,1024,256]{2,0,1:T(8,128)(2,1)}) %all-gather.7.cloned.1.call-update) | async-done | bytes 8388624 | tf_op jit(solution)/shard_map/all_gather | solution.py:42
  66.4 3.9 gather_fusion
  70.3 3.4 fusion.72
  81.6 3.6 fusion.16
  85.2 42.1 %all-gather.9.cloned.1.call-done = bf16[16,1024,256]{2,0,1:T(8,128)(2,1)} async-done(((bf16[16,32,256]{2,0,1:T(8,128)(2,1)}), bf16[16,1024,256]{2,0,1:T(8,128)(2,1)}) %all-gather.9.cloned.1.call-update) | async-done | bytes 8388624 | tf_op jit(solution)/shard_map/all_gather | solution.py:42
  127.3 3.9 gather_fusion.1
  131.2 3.4 fusion.6
  134.7 3.4 fusion.141
  145.9 3.6 fusion.14
  149.6 42.1 %all-gather.11.cloned.1.call-done = bf16[16,1024,256]{2,0,1:T(8,128)(2,1)} async-done(((bf16[16,32,256]{2,0,1:T(8,128)(2,1)}), bf16[16,1024,256]{2,0,1:T(8,128)(2,1)}) %all-gather.11.cloned.1.call-update) | async-done | bytes 8388624 | tf_op jit(solution)/shard_map/all_gather | solution.py:42
  191.6 3.9 gather_fusion.2
  195.6 3.4 fusion.4
  199.0 3.4 fusion.129
  210.3 3.6 fusion.12
  213.9 42.1 %all-gather.13.cloned.1.call-done = bf16[16,1024,256]{2,0,1:T(8,128)(2,1)} async-done(((bf16[16,32,256]{2,0,1:T(8,128)(2,1)}), bf16[16,1024,256]{2,0,1:T(8,128)(2,1)}) %all-gather.13.cloned.1.call-update) | async-done | bytes 8388624 | tf_op jit(solution)/shard_map/all_gather | solution.py:42
  256.0 3.9 gather_fusion.3
  259.9 3.4 fusion.2
  263.3 3.4 fusion.117
  275.5 3.8 fusion.10
  279.3 18.8 %all-gather.15.cloned.1.call-done = f32[64,8192]{1,0:T(8,128)} async-done(((f32[16,8192]{1,0:T(8,128)}), f32[64,8192]{1,0:T(8,128)}) %all-gather.15.cloned.1.call-update) | async-done | bytes 2097168 | tf_op jit(solution)/shard_map/all_gather | solution.py:55
  301.5 51.9 %all-gather.17.cloned.1.call-done = bf16[16,1024,256]{2,0,1:T(8,128)(2,1)} async-done(((bf16[16,32,256]{2,0,1:T(8,128)(2,1)}), bf16[16,1024,256]{2,0,1:T(8,128)(2,1)}) %all-gather.17.cloned.1.call-update) | async-done | bytes 8388624 | tf_op jit(solution)/shard_map/all_gather | solution.py:42
  353.3 3.9 gather_fusion.4
  357.3 3.4 fusion
  360.7 3.6 fusion.105
  366.1 126.6 %all-reduce = (f32[64,16]{0,1:T(8,128)S(1)}, f32[64,16]{0,1:T(8,128)S(1)}) all-reduce(f32[64,16]{0,1:T(8,128)S(1)} %fusion.239, f32[64,16]{0,1:T(8,128)S(1)} %fusion.240), channel_id=1, replica_groups=mesh['rows'=32,'cols'=4] {'rows'}, use_global_device_ids=true, to_apply=%region_0.2 | all-reduce | flops 2048 | bytes 16384 | tf_op jit(solution)/shard_map/psum | solution.py:59
  492.6 12.4 %all_gather.29 = f32[64,64]{0,1:T(8,128)S(1)} all-gather(f32[64,16]{0,1:T(8,128)S(1)} %get-tuple-element.3), channel_id=1, replica_groups=mesh['rows'=32,'cols'=4] {'cols'}, dimensions={1}, use_global_device_ids=true | all-gather | bytes 20480 | tf_op jit(solution)/shard_map/all_gather | solution.py:60
  505.2 5.8 %cholesky.17 = f32[64,64]{1,0:T(8,128)S(1)} custom-call(f32[64,64]{1,0:T(8,128)S(1)} %fusion.202), custom_call_target="Cholesky" | custom-call | tf_op jit(solution)/shard_map/jit(cholesky)/cholesky | solution.py:65
  512.4 4.9 custom-call.6
  517.5 11.9 %all_gather.31 = f32[64,64]{0,1:T(8,128)S(1)} all-gather(f32[64,16]{0,1:T(8,128)S(1)} %get-tuple-element.4), channel_id=1, replica_groups=mesh['rows'=32,'cols'=4] {'cols'}, dimensions={1}, use_global_device_ids=true | all-gather | bytes 20480 | tf_op jit(solution)/shard_map/all_gather | solution.py:64
  (87 shorter events, 48.5 us)
Async XLA Ops:
  7.2 59.2 %all-gather.7.cloned.1.call-start = ((), (), s32[]{:S(2)}) async-start(), calls=%async_computation | async-start | bytes 8650752 | tf_op jit(solution)/shard_map/all_gather | solution.py:42
  9.0 118.3 %all-gather.9.cloned.1.call-start = ((), (), s32[]{:S(2)}) async-start(), calls=%async_computation.1 | async-start | bytes 8650752 | tf_op jit(solution)/shard_map/all_gather | solution.py:42
  9.8 10.1 %collective-permute-start = (bf16[16,1,256]{2,0,1:T(8,128)(2,1)S(1)}, bf16[16,1,256]{2,0,1:T(8,128)(2,1)S(1)}, u32[]{:S(2)}, u32[]{:S(2)}) collective-permute-start(bf16[16,1,256]{2,0,1:T(8,128)(2,1)S(1)} %get-tuple-element.24), channel_id=1, source_target_pairs={{0,4},{4,8},{8,12},{12,16},{16,20},{20,24},{24,28},{28,32},{32,36}... | collective-permute-start | bytes 24584 | tf_op jit(solution)/shard_map/ppermute | solution.py:15
  9.8 13.7 %collective-permute-start.1 = (bf16[16,1,256]{2,0,1:T(8,128)(2,1)S(1)}, bf16[16,1,256]{2,0,1:T(8,128)(2,1)S(1)}, u32[]{:S(2)}, u32[]{:S(2)}) collective-permute-start(bf16[16,1,256]{2,0,1:T(8,128)(2,1)S(1)} %get-tuple-element.23), channel_id=1, source_target_pairs={{4,0},{8,4},{12,8},{16,12},{20,16},{24,20},{28,24},{32,28},{36,32}... | collective-permute-start | bytes 24584 | tf_op jit(solution)/shard_map/ppermute | solution.py:18
  19.9 3.6 copy-start.4
  23.5 50.3 %copy-start.2 = (f32[16,8192]{1,0:T(8,128)S(1)}, f32[16,8192]{1,0:T(8,128)}, u32[]{:S(2)}) copy-start(f32[16,8192]{1,0:T(8,128)} %param.5) | copy-start | bytes 1572868
  74.6 117.0 %all-gather.11.cloned.1.call-start = ((), (), s32[]{:S(2)}) async-start(), calls=%async_computation.2 | async-start | bytes 8650752 | tf_op jit(solution)/shard_map/all_gather | solution.py:42
  75.4 6.2 %collective-permute-start.3 = (bf16[16,1,256]{2,0,1:T(8,128)(2,1)S(1)}, bf16[16,1,256]{2,0,1:T(8,128)(2,1)S(1)}, u32[]{:S(2)}, u32[]{:S(2)}) collective-permute-start(bf16[16,1,256]{2,0,1:T(8,128)(2,1)S(1)} %get-tuple-element.22), channel_id=1, source_target_pairs={{4,0},{8,4},{12,8},{16,12},{20,16},{24,20},{28,24},{32,28},{36,32}... | collective-permute-start | bytes 24584 | tf_op jit(solution)/shard_map/ppermute | solution.py:18
  81.6 53.1 %copy-start.5 = (bf16[2,32,8,256]{3,2,0,1:T(8,128)(2,1)S(1)}, bf16[2,32,8,256]{3,2,0,1:T(8,128)(2,1)}, u32[]{:S(2)}) copy-start(bf16[2,32,8,256]{3,2,0,1:T(8,128)(2,1)} %copy.157) | copy-start | bytes 786436
  81.6 53.1 %collective-permute-start.2 = (bf16[16,1,256]{2,0,1:T(8,128)(2,1)S(1)}, bf16[16,1,256]{2,0,1:T(8,128)(2,1)S(1)}, u32[]{:S(2)}, u32[]{:S(2)}) collective-permute-start(bf16[16,1,256]{2,0,1:T(8,128)(2,1)S(1)} %get-tuple-element.21), channel_id=1, source_target_pairs={{0,4},{4,8},{8,12},{12,16},{16,20},{20,24},{24,28},{28,32},{32,36}... | collective-permute-start | bytes 24584 | tf_op jit(solution)/shard_map/ppermute | solution.py:15
  138.9 117.0 %all-gather.13.cloned.1.call-start = ((), (), s32[]{:S(2)}) async-start(), calls=%async_computation.3 | async-start | bytes 8650752 | tf_op jit(solution)/shard_map/all_gather | solution.py:42
  139.7 6.2 %collective-permute-start.5 = (bf16[16,1,256]{2,0,1:T(8,128)(2,1)S(1)}, bf16[16,1,256]{2,0,1:T(8,128)(2,1)S(1)}, u32[]{:S(2)}, u32[]{:S(2)}) collective-permute-start(bf16[16,1,256]{2,0,1:T(8,128)(2,1)S(1)} %get-tuple-element.20), channel_id=1, source_target_pairs={{4,0},{8,4},{12,8},{16,12},{20,16},{24,20},{28,24},{32,28},{36,32}... | collective-permute-start | bytes 24584 | tf_op jit(solution)/shard_map/ppermute | solution.py:18
  145.9 53.1 %copy-start.6 = (bf16[2,32,8,256]{3,2,0,1:T(8,128)(2,1)S(1)}, bf16[2,32,8,256]{3,2,0,1:T(8,128)(2,1)}, u32[]{:S(2)}) copy-start(bf16[2,32,8,256]{3,2,0,1:T(8,128)(2,1)} %copy.156) | copy-start | bytes 786436
  145.9 53.1 %collective-permute-start.4 = (bf16[16,1,256]{2,0,1:T(8,128)(2,1)S(1)}, bf16[16,1,256]{2,0,1:T(8,128)(2,1)S(1)}, u32[]{:S(2)}, u32[]{:S(2)}) collective-permute-start(bf16[16,1,256]{2,0,1:T(8,128)(2,1)S(1)} %get-tuple-element.19), channel_id=1, source_target_pairs={{0,4},{4,8},{8,12},{12,16},{16,20},{20,24},{24,28},{28,32},{32,36}... | collective-permute-start | bytes 24584 | tf_op jit(solution)/shard_map/ppermute | solution.py:15
  203.3 94.9 %all-gather.15.cloned.1.call-start = ((), (), s32[]{:S(2)}) async-start(), calls=%async_computation.4 | async-start | bytes 2621440 | tf_op jit(solution)/shard_map/all_gather | solution.py:55
  204.0 6.2 %collective-permute-start.7 = (bf16[16,1,256]{2,0,1:T(8,128)(2,1)S(1)}, bf16[16,1,256]{2,0,1:T(8,128)(2,1)S(1)}, u32[]{:S(2)}, u32[]{:S(2)}) collective-permute-start(bf16[16,1,256]{2,0,1:T(8,128)(2,1)S(1)} %get-tuple-element.18), channel_id=1, source_target_pairs={{4,0},{8,4},{12,8},{16,12},{20,16},{24,20},{28,24},{32,28},{36,32}... | collective-permute-start | bytes 24584 | tf_op jit(solution)/shard_map/ppermute | solution.py:18
  210.3 53.1 %copy-start.7 = (bf16[2,32,8,256]{3,2,0,1:T(8,128)(2,1)S(1)}, bf16[2,32,8,256]{3,2,0,1:T(8,128)(2,1)}, u32[]{:S(2)}) copy-start(bf16[2,32,8,256]{3,2,0,1:T(8,128)(2,1)} %copy.155) | copy-start | bytes 786436
  210.3 53.1 %collective-permute-start.6 = (bf16[16,1,256]{2,0,1:T(8,128)(2,1)S(1)}, bf16[16,1,256]{2,0,1:T(8,128)(2,1)S(1)}, u32[]{:S(2)}, u32[]{:S(2)}) collective-permute-start(bf16[16,1,256]{2,0,1:T(8,128)(2,1)S(1)} %get-tuple-element.17), channel_id=1, source_target_pairs={{0,4},{4,8},{8,12},{12,16},{16,20},{20,24},{24,28},{28,32},{32,36}... | collective-permute-start | bytes 24584 | tf_op jit(solution)/shard_map/ppermute | solution.py:15
  267.7 85.7 %all-gather.17.cloned.1.call-start = ((), (), s32[]{:S(2)}) async-start(), calls=%async_computation.5 | async-start | bytes 8650752 | tf_op jit(solution)/shard_map/all_gather | solution.py:42
  269.2 6.2 %collective-permute-start.9 = (bf16[16,1,256]{2,0,1:T(8,128)(2,1)S(1)}, bf16[16,1,256]{2,0,1:T(8,128)(2,1)S(1)}, u32[]{:S(2)}, u32[]{:S(2)}) collective-permute-start(bf16[16,1,256]{2,0,1:T(8,128)(2,1)S(1)} %get-tuple-element.16), channel_id=1, source_target_pairs={{4,0},{8,4},{12,8},{16,12},{20,16},{24,20},{28,24},{32,28},{36,32}... | collective-permute-start | bytes 24584 | tf_op jit(solution)/shard_map/ppermute | solution.py:18
  275.4 22.7 %copy-start.1 = (f32[16,8192]{1,0:T(8,128)S(1)}, f32[16,8192]{1,0:T(8,128)}, u32[]{:S(2)}) copy-start(f32[16,8192]{1,0:T(8,128)} %get-tuple-element.6) | copy-start | bytes 1572868
  275.4 85.3 %copy-start.3 = (bf16[2,32,8,256]{3,2,0,1:T(8,128)(2,1)S(1)}, bf16[2,32,8,256]{3,2,0,1:T(8,128)(2,1)}, u32[]{:S(2)}) copy-start(bf16[2,32,8,256]{3,2,0,1:T(8,128)(2,1)} %copy.154) | copy-start | bytes 786436
  275.4 85.3 %collective-permute-start.8 = (bf16[16,1,256]{2,0,1:T(8,128)(2,1)S(1)}, bf16[16,1,256]{2,0,1:T(8,128)(2,1)S(1)}, u32[]{:S(2)}, u32[]{:S(2)}) collective-permute-start(bf16[16,1,256]{2,0,1:T(8,128)(2,1)S(1)} %get-tuple-element.15), channel_id=1, source_target_pairs={{0,4},{4,8},{8,12},{12,16},{16,20},{20,24},{24,28},{28,32},{32,36}... | collective-permute-start | bytes 24584 | tf_op jit(solution)/shard_map/ppermute | solution.py:15
  360.7 3.6 copy-start
Sparse Core Ops, SparseCore 0:
  10.8 55.4 all-gather.6
  74.7 52.5 all-gather.8
  139.1 52.5 all-gather.10
  203.4 52.5 all-gather.12
  267.8 30.2 all-gather.14
  300.2 53.0 all-gather.16
where the time goes:
time: 540 us; the launch traced here: 539 us
  waiting for transfers between devices  236 us (44%)
  blocking collectives  151 us (28%)
  matrix products  77.1 us (14%)
  local copies, waits for them, and re-layouts  27.9 us (5%)
  starting transfers between devices  17.6 us (3%)
  other arithmetic  14.9 us (3%)
  between operations  14.4 us (3%)
    all_gather x5, waiting for transfers between devices, apply_generator(): piece = lax.all_gather(shaped, 'rows', axis=1, tiled=True)  217 us
    psum x1, blocking collectives, body(): gram_mine = lax.psum(gram_part, 'rows')  127 us
    dot_general x20, matrix products, block_product(): jnp.einsum('jbt,bst->jbs', pieces, blocks[:, position], preferred_element...  69.5 us
    gather x5, local copies, waits for them, and re-layouts, apply_generator(): taken = jnp.take(piece, jnp.clip(far_cols, 0, piece.shape[1] - 1), axis=1)  19.7 us
    all_gather x1, waiting for transfers between devices, body(): whole_iterate = lax.all_gather(iterate, 'cols', axis=0, tiled=True)  18.8 us
    ppermute x5, starting transfers between devices, with_halo(): lax.ppermute(lax.slice_in_dim(block, 0, width, axis=dim), axis, backward)  17.3 us
    all_gather x1, blocking collectives, body(): gram = lax.all_gather(gram_mine, 'cols', axis=1, tiled=True) / total_states  12.4 us
    all_gather x1, blocking collectives, body(): lax.all_gather(product_mine, 'cols', axis=1, tiled=True) / total_states  11.9 us
  transfers between devices with their start and end apart: 16, of which 6 were waited for; matrix products, arithmetic and copies ran while one was open for 14% of the time, Pallas kernels for 0%

commit v1 on v0

--- a/solution.py
+++ b/solution.py
@@ -56,7 +56,11 @@
     contract = (((1,), (1,)), ((), ()))
     gram_part = lax.dot_general(whole_iterate, iterate, contract, precision=highest)
     column_start = lax.axis_index("cols") * width
-    gram_mine = lax.psum(gram_part, "rows")
+    gram_mine = gram_part
+    for hop in (1, 2, 4, 8, 16):
+        gram_mine = gram_mine + lax.ppermute(
+            gram_mine, "rows", [(dev, dev ^ hop) for dev in range(32)]
+        )
     gram = lax.all_gather(gram_mine, "cols", axis=1, tiled=True) / total_states
     applied = apply_generator(iterate.astype(jnp.bfloat16))
     product_part = lax.dot_general(whole_iterate, applied, contract, precision=highest)

time: 540 us -> 454 us (0.84)
  blocking collectives: 151 us -> 91 us
  waiting for transfers between devices: 236 us -> 202 us
  starting transfers between devices: 17.6 us -> 25.1 us
    psum x1, blocking collectives: 127 us -> 66.5 us  [body(): product_mine = lax.psum(product_part, 'rows')]
    all_gather x5, waiting for transfers between devices: 217 us -> 168 us  [apply_generator(): piece = lax.all_gather(shaped, 'rows', axis=1, tiled=True)]
    all_gather x1, waiting for transfers between devices: 18.8 us -> 29.7 us  [body(): whole_iterate = lax.all_gather(iterate, 'cols', axis=0, tiled=True)]
    ppermute x0 -> x5, starting transfers between devices: none -> 8.52 us  [body(): lax.ppermute(gram_mine, 'rows', [(dev, dev ^ hop) for dev in range(32)])]
  transfers between devices with their start and end apart: 16 -> 21, of which waited for: 6 -> 8; matrix products, arithmetic and copies ran while one was open for 14% -> 20% of each run, Pallas kernels for 0% -> 0%
where the time goes in v1:
time: 454 us; the launch traced here: 453 us
  waiting for transfers between devices  202 us (44%)
  blocking collectives  91 us (20%)
  matrix products  77.7 us (17%)
  local copies, waits for them, and re-layouts  27.9 us (6%)
  starting transfers between devices  25.1 us (6%)
  other arithmetic  14.9 us (3%)
  between operations  14.5 us (3%)
    all_gather x5, waiting for transfers between devices, apply_generator(): piece = lax.all_gather(shaped, 'rows', axis=1, tiled=True)  168 us
    dot_general x20, matrix products, block_product(): jnp.einsum('jbt,bst->jbs', pieces, blocks[:, position], preferred_element...  70 us
    psum x1, blocking collectives, body(): product_mine = lax.psum(product_part, 'rows')  66.5 us
    all_gather x1, waiting for transfers between devices, body(): whole_iterate = lax.all_gather(iterate, 'cols', axis=0, tiled=True)  29.7 us
    gather x5, local copies, waits for them, and re-layouts, apply_generator(): taken = jnp.take(piece, jnp.clip(far_cols, 0, piece.shape[1] - 1), axis=1)  19.7 us
    ppermute x5, starting transfers between devices, with_halo(): lax.ppermute(lax.slice_in_dim(block, 0, width, axis=dim), axis, backward)  16.3 us
    all_gather x1, blocking collectives, body(): lax.all_gather(product_mine, 'cols', axis=1, tiled=True) / total_states  12.3 us
    all_gather x1, blocking collectives, body(): gram = lax.all_gather(gram_mine, 'cols', axis=1, tiled=True) / total_states  12.3 us
  transfers between devices with their start and end apart: 21, of which 8 were waited for; matrix products, arithmetic and copies ran while one was open for 20% of the time, Pallas kernels for 0%

profile of v1, /device:TPU:0, one launch (start us, length us, event | category | flops | bytes accessed | tf_op | source)
XLA Modules:
  0.0 452.6 jit_solution(7255846742896969997)
XLA Ops:
  9.8 6.0 %collective-permute-start.1 = (bf16[16,1,256]{2,0,1:T(8,128)(2,1)S(1)}, bf16[16,1,256]{2,0,1:T(8,128)(2,1)S(1)}, u32[]{:S(2)}, u32[]{:S(2)}) collective-permute-start(bf16[16,1,256]{2,0,1:T(8,128)(2,1)S(1)} %get-tuple-element.21), channel_id=1, source_target_pairs={{4,0},{8,4},{12,8},{16,12},{20,16},{24,20},{28,24},{32,28},{36,32}... | collective-permute-start | bytes 24584 | tf_op jit(solution)/shard_map/ppermute | solution.py:18
  19.9 3.6 fusion.84
  23.5 3.5 fusion.81
  27.0 39.3 %all-gather.7.cloned.1.call-done = bf16[16,1024,256]{2,0,1:T(8,128)(2,1)} async-done(((bf16[16,32,256]{2,0,1:T(8,128)(2,1)}), bf16[16,1024,256]{2,0,1:T(8,128)(2,1)}) %all-gather.7.cloned.1.call-update) | async-done | bytes 8388624 | tf_op jit(solution)/shard_map/all_gather | solution.py:42
  66.4 3.9 gather_fusion
  70.3 3.4 fusion.72
  78.2 3.4 fusion.36
  81.6 3.6 fusion.16
  85.2 42.1 %all-gather.9.cloned.1.call-done = bf16[16,1024,256]{2,0,1:T(8,128)(2,1)} async-done(((bf16[16,32,256]{2,0,1:T(8,128)(2,1)}), bf16[16,1024,256]{2,0,1:T(8,128)(2,1)}) %all-gather.9.cloned.1.call-update) | async-done | bytes 8388624 | tf_op jit(solution)/shard_map/all_gather | solution.py:42
  127.3 3.9 gather_fusion.1
  131.2 3.4 fusion.6
  134.7 3.4 fusion.141
  145.9 3.6 fusion.14
  149.6 42.1 %all-gather.11.cloned.1.call-done = bf16[16,1024,256]{2,0,1:T(8,128)(2,1)} async-done(((bf16[16,32,256]{2,0,1:T(8,128)(2,1)}), bf16[16,1024,256]{2,0,1:T(8,128)(2,1)}) %all-gather.11.cloned.1.call-update) | async-done | bytes 8388624 | tf_op jit(solution)/shard_map/all_gather | solution.py:42
  191.6 3.9 gather_fusion.2
  199.0 3.4 fusion.129
  210.3 3.6 fusion.12
  213.9 42.1 %all-gather.13.cloned.1.call-done = bf16[16,1024,256]{2,0,1:T(8,128)(2,1)} async-done(((bf16[16,32,256]{2,0,1:T(8,128)(2,1)}), bf16[16,1024,256]{2,0,1:T(8,128)(2,1)}) %all-gather.13.cloned.1.call-update) | async-done | bytes 8388624 | tf_op jit(solution)/shard_map/all_gather | solution.py:42
  256.0 3.9 gather_fusion.3
  259.9 3.4 fusion.2
  263.3 3.4 fusion.117
  268.5 29.7 %all-gather.15.cloned.1.call-done = f32[64,8192]{1,0:T(8,128)} async-done(((f32[16,8192]{1,0:T(8,128)}), f32[64,8192]{1,0:T(8,128)}) %all-gather.15.cloned.1.call-update) | async-done | bytes 2097168 | tf_op jit(solution)/shard_map/all_gather | solution.py:55
  298.1 3.4 fusion.239
  319.4 4.4 fusion.10
  323.8 12.3 %all_gather.29 = f32[64,64]{0,1:T(8,128)S(1)} all-gather(f32[64,16]{0,1:T(8,128)S(1)} %add.129), channel_id=1, replica_groups=mesh['rows'=32,'cols'=4] {'cols'}, dimensions={1}, use_global_device_ids=true | all-gather | bytes 20480 | tf_op jit(solution)/shard_map/all_gather | solution.py:64
  336.2 5.8 %cholesky.17 = f32[64,64]{1,0:T(8,128)S(1)} custom-call(f32[64,64]{1,0:T(8,128)S(1)} %fusion.202), custom_call_target="Cholesky" | custom-call | tf_op jit(solution)/shard_map/jit(cholesky)/cholesky | solution.py:69
  343.4 4.9 %custom-call.6 = f32[1,64,64]{1,2,0:T(8,128)S(1)} custom-call(f32[1,64,64]{2,1,0:T(8,128)S(1)} %fusion.199), custom_call_target="InvertDiagBlocksLowerTriangular" | custom-call | tf_op jit(solution)/shard_map/triangular_solve | solution.py:71
  353.3 3.9 gather_fusion.4
  357.3 3.4 fusion
  360.7 3.5 fusion.105
  366.0 66.5 %psum.7 = f32[64,16]{0,1:T(8,128)S(1)} all-reduce(f32[64,16]{0,1:T(8,128)S(1)} %fusion.240), channel_id=1, replica_groups=mesh['rows'=32,'cols'=4] {'rows'}, use_global_device_ids=true, to_apply=%region_2.4 | all-reduce | flops 1024 | bytes 8192 | tf_op jit(solution)/shard_map/psum | solution.py:67
  432.5 12.3 %all_gather.31 = f32[64,64]{0,1:T(8,128)S(1)} all-gather(f32[64,16]{0,1:T(8,128)S(1)} %psum.7), channel_id=1, replica_groups=mesh['rows'=32,'cols'=4] {'cols'}, dimensions={1}, use_global_device_ids=true | all-gather | bytes 20480 | tf_op jit(solution)/shard_map/all_gather | solution.py:68
  (100 shorter events, 59.0 us)
Async XLA Ops:
  7.2 59.2 %all-gather.7.cloned.1.call-start = ((), (), s32[]{:S(2)}) async-start(), calls=%async_computation | async-start | bytes 8650752 | tf_op jit(solution)/shard_map/all_gather | solution.py:42
  9.0 118.3 %all-gather.9.cloned.1.call-start = ((), (), s32[]{:S(2)}) async-start(), calls=%async_computation.1 | async-start | bytes 8650752 | tf_op jit(solution)/shard_map/all_gather | solution.py:42
  9.8 10.1 %collective-permute-start = (bf16[16,1,256]{2,0,1:T(8,128)(2,1)S(1)}, bf16[16,1,256]{2,0,1:T(8,128)(2,1)S(1)}, u32[]{:S(2)}, u32[]{:S(2)}) collective-permute-start(bf16[16,1,256]{2,0,1:T(8,128)(2,1)S(1)} %get-tuple-element.22), channel_id=1, source_target_pairs={{0,4},{4,8},{8,12},{12,16},{16,20},{20,24},{24,28},{28,32},{32,36}... | collective-permute-start | bytes 24584 | tf_op jit(solution)/shard_map/ppermute | solution.py:15
  9.8 13.7 %collective-permute-start.1 = (bf16[16,1,256]{2,0,1:T(8,128)(2,1)S(1)}, bf16[16,1,256]{2,0,1:T(8,128)(2,1)S(1)}, u32[]{:S(2)}, u32[]{:S(2)}) collective-permute-start(bf16[16,1,256]{2,0,1:T(8,128)(2,1)S(1)} %get-tuple-element.21), channel_id=1, source_target_pairs={{4,0},{8,4},{12,8},{16,12},{20,16},{24,20},{28,24},{32,28},{36,32}... | collective-permute-start | bytes 24584 | tf_op jit(solution)/shard_map/ppermute | solution.py:18
  19.9 3.6 copy-start.3
  23.5 50.3 %copy-start.1 = (f32[16,8192]{1,0:T(8,128)S(1)}, f32[16,8192]{1,0:T(8,128)}, u32[]{:S(2)}) copy-start(f32[16,8192]{1,0:T(8,128)} %param.5) | copy-start | bytes 1572868
  74.6 117.0 %all-gather.11.cloned.1.call-start = ((), (), s32[]{:S(2)}) async-start(), calls=%async_computation.2 | async-start | bytes 8650752 | tf_op jit(solution)/shard_map/all_gather | solution.py:42
  75.4 6.2 %collective-permute-start.3 = (bf16[16,1,256]{2,0,1:T(8,128)(2,1)S(1)}, bf16[16,1,256]{2,0,1:T(8,128)(2,1)S(1)}, u32[]{:S(2)}, u32[]{:S(2)}) collective-permute-start(bf16[16,1,256]{2,0,1:T(8,128)(2,1)S(1)} %get-tuple-element.20), channel_id=1, source_target_pairs={{4,0},{8,4},{12,8},{16,12},{20,16},{24,20},{28,24},{32,28},{36,32}... | collective-permute-start | bytes 24584 | tf_op jit(solution)/shard_map/ppermute | solution.py:18
  81.6 53.1 %copy-start.4 = (bf16[2,32,8,256]{3,2,0,1:T(8,128)(2,1)S(1)}, bf16[2,32,8,256]{3,2,0,1:T(8,128)(2,1)}, u32[]{:S(2)}) copy-start(bf16[2,32,8,256]{3,2,0,1:T(8,128)(2,1)} %copy.157) | copy-start | bytes 786436
  81.6 53.1 %collective-permute-start.2 = (bf16[16,1,256]{2,0,1:T(8,128)(2,1)S(1)}, bf16[16,1,256]{2,0,1:T(8,128)(2,1)S(1)}, u32[]{:S(2)}, u32[]{:S(2)}) collective-permute-start(bf16[16,1,256]{2,0,1:T(8,128)(2,1)S(1)} %get-tuple-element.19), channel_id=1, source_target_pairs={{0,4},{4,8},{8,12},{12,16},{16,20},{20,24},{24,28},{28,32},{32,36}... | collective-permute-start | bytes 24584 | tf_op jit(solution)/shard_map/ppermute | solution.py:15
  138.9 117.0 %all-gather.13.cloned.1.call-start = ((), (), s32[]{:S(2)}) async-start(), calls=%async_computation.3 | async-start | bytes 8650752 | tf_op jit(solution)/shard_map/all_gather | solution.py:42
  139.7 6.2 %collective-permute-start.5 = (bf16[16,1,256]{2,0,1:T(8,128)(2,1)S(1)}, bf16[16,1,256]{2,0,1:T(8,128)(2,1)S(1)}, u32[]{:S(2)}, u32[]{:S(2)}) collective-permute-start(bf16[16,1,256]{2,0,1:T(8,128)(2,1)S(1)} %get-tuple-element.18), channel_id=1, source_target_pairs={{4,0},{8,4},{12,8},{16,12},{20,16},{24,20},{28,24},{32,28},{36,32}... | collective-permute-start | bytes 24584 | tf_op jit(solution)/shard_map/ppermute | solution.py:18
  145.9 53.1 %copy-start.5 = (bf16[2,32,8,256]{3,2,0,1:T(8,128)(2,1)S(1)}, bf16[2,32,8,256]{3,2,0,1:T(8,128)(2,1)}, u32[]{:S(2)}) copy-start(bf16[2,32,8,256]{3,2,0,1:T(8,128)(2,1)} %copy.156) | copy-start | bytes 786436
  145.9 53.1 %collective-permute-start.4 = (bf16[16,1,256]{2,0,1:T(8,128)(2,1)S(1)}, bf16[16,1,256]{2,0,1:T(8,128)(2,1)S(1)}, u32[]{:S(2)}, u32[]{:S(2)}) collective-permute-start(bf16[16,1,256]{2,0,1:T(8,128)(2,1)S(1)} %get-tuple-element.17), channel_id=1, source_target_pairs={{0,4},{4,8},{8,12},{12,16},{16,20},{20,24},{24,28},{28,32},{32,36}... | collective-permute-start | bytes 24584 | tf_op jit(solution)/shard_map/ppermute | solution.py:15
  203.3 94.9 %all-gather.15.cloned.1.call-start = ((), (), s32[]{:S(2)}) async-start(), calls=%async_computation.4 | async-start | bytes 2621440 | tf_op jit(solution)/shard_map/all_gather | solution.py:55
  204.0 6.2 %collective-permute-start.7 = (bf16[16,1,256]{2,0,1:T(8,128)(2,1)S(1)}, bf16[16,1,256]{2,0,1:T(8,128)(2,1)S(1)}, u32[]{:S(2)}, u32[]{:S(2)}) collective-permute-start(bf16[16,1,256]{2,0,1:T(8,128)(2,1)S(1)} %get-tuple-element.16), channel_id=1, source_target_pairs={{4,0},{8,4},{12,8},{16,12},{20,16},{24,20},{28,24},{32,28},{36,32}... | collective-permute-start | bytes 24584 | tf_op jit(solution)/shard_map/ppermute | solution.py:18
  210.3 53.1 %copy-start.6 = (bf16[2,32,8,256]{3,2,0,1:T(8,128)(2,1)S(1)}, bf16[2,32,8,256]{3,2,0,1:T(8,128)(2,1)}, u32[]{:S(2)}) copy-start(bf16[2,32,8,256]{3,2,0,1:T(8,128)(2,1)} %copy.155) | copy-start | bytes 786436
  210.3 53.1 %collective-permute-start.6 = (bf16[16,1,256]{2,0,1:T(8,128)(2,1)S(1)}, bf16[16,1,256]{2,0,1:T(8,128)(2,1)S(1)}, u32[]{:S(2)}, u32[]{:S(2)}) collective-permute-start(bf16[16,1,256]{2,0,1:T(8,128)(2,1)S(1)} %get-tuple-element.15), channel_id=1, source_target_pairs={{0,4},{4,8},{8,12},{12,16},{16,20},{20,24},{24,28},{28,32},{32,36}... | collective-permute-start | bytes 24584 | tf_op jit(solution)/shard_map/ppermute | solution.py:15
  267.7 85.7 %all-gather.17.cloned.1.call-start = ((), (), s32[]{:S(2)}) async-start(), calls=%async_computation.5 | async-start | bytes 8650752 | tf_op jit(solution)/shard_map/all_gather | solution.py:42
  301.5 1.2 collective-permute-start.8
  302.7 3.7 collective-permute-start.9
  306.4 5.6 %collective-permute-start.10 = (f32[64,16]{0,1:T(8,128)S(1)}, f32[64,16]{0,1:T(8,128)S(1)}, u32[]{:S(2)}, u32[]{:S(2)}) collective-permute-start(f32[64,16]{0,1:T(8,128)S(1)} %add.126), channel_id=1, source_target_pairs={{0,16},{4,20},{8,24},{12,28},{16,0},{20,4},{24,8},{28,12},{32,48},... | collective-permute-start | bytes 12296 | tf_op jit(solution)/shard_map/ppermute | solution.py:61
  310.1 9.3 %collective-permute-start.14 = (bf16[16,1,256]{2,0,1:T(8,128)(2,1)S(1)}, bf16[16,1,256]{2,0,1:T(8,128)(2,1)S(1)}, u32[]{:S(2)}, u32[]{:S(2)}) collective-permute-start(bf16[16,1,256]{2,0,1:T(8,128)(2,1)S(1)} %get-tuple-element.14), channel_id=1, source_target_pairs={{4,0},{8,4},{12,8},{16,12},{20,16},{24,20},{28,24},{32,28},{36,32}... | collective-permute-start | bytes 24584 | tf_op jit(solution)/shard_map/ppermute | solution.py:18
  312.0 4.5 collective-permute-start.11
  316.5 44.2 %collective-permute-start.13 = (bf16[16,1,256]{2,0,1:T(8,128)(2,1)S(1)}, bf16[16,1,256]{2,0,1:T(8,128)(2,1)S(1)}, u32[]{:S(2)}, u32[]{:S(2)}) collective-permute-start(bf16[16,1,256]{2,0,1:T(8,128)(2,1)S(1)} %get-tuple-element.13), channel_id=1, source_target_pairs={{0,4},{4,8},{8,12},{12,16},{16,20},{20,24},{24,28},{28,32},{32,36}... | collective-permute-start | bytes 24584 | tf_op jit(solution)/shard_map/ppermute | solution.py:15
  316.5 32.0 %copy-start = (f32[64,8192]{1,0:T(8,128)S(1)}, f32[64,8192]{1,0:T(8,128)}, u32[]{:S(2)}) copy-start(f32[64,8192]{1,0:T(8,128)} %all-gather.15.cloned.1.call-done) | copy-start | bytes 6291460
  316.5 7.3 %collective-permute-start.12 = (f32[64,16]{0,1:T(8,128)S(1)}, f32[64,16]{0,1:T(8,128)S(1)}, u32[]{:S(2)}, u32[]{:S(2)}) collective-permute-start(f32[64,16]{0,1:T(8,128)S(1)} %add.128), channel_id=1, source_target_pairs={{0,64},{4,68},{8,72},{12,76},{16,80},{20,84},{24,88},{28,92},{32,9... | collective-permute-start | bytes 12296 | tf_op jit(solution)/shard_map/ppermute | solution.py:61
  323.8 36.9 %copy-start.2 = (bf16[2,32,8,256]{3,2,0,1:T(8,128)(2,1)S(1)}, bf16[2,32,8,256]{3,2,0,1:T(8,128)(2,1)}, u32[]{:S(2)}) copy-start(bf16[2,32,8,256]{3,2,0,1:T(8,128)(2,1)} %copy.154) | copy-start | bytes 786436
Sparse Core Ops, SparseCore 0:
  10.8 55.4 all-gather.6
  74.7 52.5 all-gather.8
  139.1 52.5 all-gather.10
  203.4 52.5 all-gather.12
  267.8 30.2 all-gather.14
  300.2 53.0 all-gather.16
